TPU v7x, 32 devices: a whole 2x2x4 slice. The times are simulated.
32 devices in a mesh: groups: 2 (over x), ctx: 2 (over core), fsdp: 8 (over z, y).
Axes of the slice: x: 2, y: 2, z: 4, core: 2. Of those that a mesh axis runs over, the one named last changes fastest.
Arguments:
- hidden_in: bfloat16 [8192, 2048], P(('groups', 'ctx', 'fsdp')), parts along dimension 0, may hold values from -6 to 6
- qkv_weight: bfloat16 [2048, 4096], P(None, 'fsdp'), may hold values from -0.125 to 0.125
- ab_weight: bfloat16 [2048, 32], replicated, may hold values from -0.125 to 0.125
- conv_weight: float32 [4, 4096], replicated, may hold values from -3 to 3
- decay_rate: float32 [16], replicated, may hold values from 7.324219e-05 to 0.3
- dt_bias: float32 [16], replicated, may hold values from -3 to -1
- norm_gain: float32 [128], replicated, may hold values from 0.1 to 1.9
- previous_tail: bfloat16 [6, 4096], P('groups'), parts along dimension 0, may hold values from -6 to 6
- window_entry_state: float32 [32, 128, 128], P('groups'), parts along dimension 0, may hold values from -3 to 3
Outputs:
- head_out: bfloat16 [8192, 2048], P(('groups', 'ctx', 'fsdp')), parts along dimension 0
There are 2 independent parts, one for each index of `groups`. A program takes and returns all parts, laid end to end along the dimension named above; an argument that names none is the same for every part. Nothing has to cross between parts.
All inputs are finite; a program needn't handle non-finite values.
Results may differ from a plain program's by a relative error of at most 0.0065.
Values may be sent and summed in bfloat16 or wider, within the bound.
A program may use at most 320 MiB of HBM per device.

v0:
```python
import jax
import jax.numpy as jnp
from jax import lax
from jax.sharding import PartitionSpec as P

HK = 8
HV = 16
DK = 128
DV = 128
SPAN = 64
exact_product = lax.Precision.HIGHEST


def shifted(array, axis, by):
    peers = lax.axis_size(axis)
    pairs = [(i, i + by) for i in range(peers) if 0 <= i + by < peers]
    return lax.ppermute(array, axis, pairs)


def entering(part, axis, combine, identity):
    place = lax.axis_index(axis)
    gathered = jax.tree.map(lambda a: lax.all_gather(a, axis), part)
    state = jax.tree.map(lambda a, e: jnp.zeros_like(a) + jnp.asarray(e, a.dtype), part, identity)

    def one(hop, state):
        return combine(
            state, jax.tree.map(lambda a: lax.dynamic_index_in_dim(a, hop, 0, False), gathered)
        )

    return lax.fori_loop(0, place, one, state)


def unit_norm(vectors):
    return vectors * lax.rsqrt(jnp.sum(vectors * vectors, axis=-1, keepdims=True) + 1e-06)


def convolve(before, mixed_qkv, conv_weight):
    length = mixed_qkv.shape[0]
    padded = jnp.concatenate([before, mixed_qkv], axis=0).astype(jnp.float32)
    summed = jnp.zeros((length, mixed_qkv.shape[1]), jnp.float32)
    for offset in range(conv_weight.shape[0]):
        summed = summed + conv_weight[offset] * padded[offset : offset + length]
    return jax.nn.silu(summed)


def to_spans(tensor, span_len):
    length, head_count = (tensor.shape[0], tensor.shape[1])
    shaped = tensor.reshape((length // span_len, span_len, head_count) + tensor.shape[2:])
    return jnp.moveaxis(shaped, 2, 1)


def head_inputs(conv_out, gate_logits, decay_rate, dt_bias):
    length = conv_out.shape[0]
    queries = unit_norm(conv_out[:, : HK * DK].reshape(length, HK, DK)) * DK ** (-0.5)
    head_keys = unit_norm(conv_out[:, HK * DK : 2 * HK * DK].reshape(length, HK, DK))
    values = conv_out[:, 2 * HK * DK :].reshape(length, HV, DV)
    queries = jnp.repeat(queries, HV // HK, axis=1)
    head_keys = jnp.repeat(head_keys, HV // HK, axis=1)
    write_rate = jax.nn.sigmoid(gate_logits[:, HV:])
    logdecay = -decay_rate * jax.nn.softplus(gate_logits[:, :HV] + dt_bias)
    return [to_spans(item, SPAN) for item in (queries, head_keys, values, write_rate, logdecay)]


def lower_inverse(strict_part):
    span_len = strict_part.shape[-1]
    unit_span = jnp.eye(span_len, dtype=strict_part.dtype)
    inverse = unit_span - strict_part
    power = strict_part
    reach = 2
    while reach < span_len:
        power = jnp.einsum("...ij,...jk->...ik", power, power, precision=exact_product)
        inverse = inverse + jnp.einsum(
            "...ij,...jk->...ik", inverse, power, precision=exact_product
        )
        reach = reach * 2
    return inverse


def span_terms(queries, head_keys, values, write_rate, logdecay):
    span_len = logdecay.shape[-1]
    cumulative = jnp.cumsum(logdecay, axis=-1)
    row_index = lax.broadcasted_iota(jnp.int32, (span_len, span_len), 0)
    col_index = lax.broadcasted_iota(jnp.int32, (span_len, span_len), 1)
    lower_mask = row_index >= col_index
    gap_log = cumulative[..., :, None] - cumulative[..., None, :]
    factor = jnp.where(lower_mask, jnp.exp(jnp.where(lower_mask, gap_log, 0.0)), 0.0)
    strict = jnp.where(row_index > col_index, factor, 0.0)
    key_products = jnp.einsum("...ik,...jk->...ij", head_keys, head_keys, precision=exact_product)
    query_products = jnp.einsum("...ik,...jk->...ij", queries, head_keys, precision=exact_product)
    inverse = lower_inverse(write_rate[..., :, None] * key_products * strict)
    growth = jnp.exp(cumulative)
    right_sides = jnp.concatenate(
        [write_rate[..., None] * values, (write_rate * growth)[..., None] * head_keys], axis=-1
    )
    solved = jnp.einsum("...ij,...jc->...ic", inverse, right_sides, precision=exact_product)
    new_values = solved[..., : values.shape[-1]]
    key_weights = solved[..., values.shape[-1] :]
    scores = query_products * factor
    window_local_output = jnp.einsum(
        "...ij,...jv->...iv", scores, new_values, precision=exact_product
    )
    effective_query = growth[..., None] * queries - jnp.einsum(
        "...ij,...jk->...ik", scores, key_weights, precision=exact_product
    )
    span_end = cumulative[..., -1]
    tail_decay = jnp.exp(span_end[..., None] - cumulative)
    decayed_keys = head_keys * tail_decay[..., None]
    unit_key = jnp.eye(head_keys.shape[-1], dtype=logdecay.dtype)
    state_mapping = jnp.exp(span_end)[..., None, None] * unit_key - jnp.einsum(
        "...ck,...cj->...kj", decayed_keys, key_weights, precision=exact_product
    )
    shifted_state = jnp.einsum(
        "...ck,...cv->...kv", decayed_keys, new_values, precision=exact_product
    )
    return (effective_query, window_local_output, state_mapping, shifted_state)


def finish(result_rows, norm_gain):
    mean_square = jnp.mean(result_rows * result_rows, axis=-1, keepdims=True)
    normed = result_rows * lax.rsqrt(mean_square + 1e-06) * norm_gain
    normed = jnp.moveaxis(normed, 1, 2)
    return normed.reshape(
        normed.shape[0] * normed.shape[1], normed.shape[2] * normed.shape[3]
    ).astype(jnp.bfloat16)


def compose(former_piece, latter_piece):
    joined_map = jnp.einsum(
        "hkj,hjm->hkm", latter_piece[0], former_piece[0], precision=exact_product
    )
    combined_state = (
        jnp.einsum("zom,zmg->zog", latter_piece[0], former_piece[1], precision=exact_product)
        + latter_piece[1]
    )
    return (joined_map, combined_state)


def shards(
    hidden_in,
    qkv_weight,
    ab_weight,
    conv_weight,
    decay_rate,
    dt_bias,
    norm_gain,
    previous_tail,
    window_entry_state,
):
    mixed_qkv = jnp.dot(
        hidden_in,
        lax.all_gather(qkv_weight, "fsdp", axis=1, tiled=True),
        preferred_element_type=jnp.float32,
    ).astype(jnp.bfloat16)
    gate_logits = jnp.dot(hidden_in, ab_weight, preferred_element_type=jnp.float32)
    tail_rows = previous_tail.shape[0]
    received = shifted(mixed_qkv[mixed_qkv.shape[0] - tail_rows :], ("ctx", "fsdp"), 1)
    before = jnp.where(lax.axis_index(("ctx", "fsdp")) == 0, previous_tail, received)
    conv_out = convolve(before, mixed_qkv, conv_weight)
    spanned = head_inputs(conv_out, gate_logits, decay_rate, dt_bias)
    effective_query, window_local_output, state_mapping, shifted_state = span_terms(*spanned)
    unit_maps = jnp.broadcast_to(jnp.eye(DK, dtype=jnp.float32), (HV, DK, DK))
    empty_state = jnp.zeros((HV, DK, DV), jnp.float32)

    def advance(carried, items):
        carry_map, carried_over_state = carried
        per_step_query, per_step_local, per_step_mapping, step_offset = items
        adjusted_result = jnp.einsum(
            "hck,hkj->hcj", per_step_query, carry_map, precision=exact_product
        )
        layer_result = per_step_local + jnp.einsum(
            "gpi,gib->gpb", per_step_query, carried_over_state, precision=exact_product
        )
        carry_map = jnp.einsum("hkj,hjm->hkm", per_step_mapping, carry_map, precision=exact_product)
        carried_over_state = (
            jnp.einsum(
                "zom,zmg->zog", per_step_mapping, carried_over_state, precision=exact_product
            )
            + step_offset
        )
        return ((carry_map, carried_over_state), (adjusted_result, layer_result))

    own_pair, (adjusted_result, incomplete_output) = lax.scan(
        advance,
        (unit_maps, empty_state),
        (effective_query, window_local_output, state_mapping, shifted_state),
    )
    identity = (unit_maps, empty_state)
    leading_pair = entering((own_pair[0], own_pair[1]), ("ctx", "fsdp"), compose, identity)
    opening_state = (
        jnp.einsum("zom,zmg->zog", leading_pair[0], window_entry_state, precision=exact_product)
        + leading_pair[1]
    )
    result_rows = incomplete_output + jnp.einsum(
        "elfx,lxw->elfw", adjusted_result, opening_state, precision=exact_product
    )
    return finish(result_rows, norm_gain)


def solution(mesh):
    placed = (
        P(("groups", "ctx", "fsdp"), None),
        P(None, "fsdp"),
        P(),
        P(),
        P(),
        P(),
        P(),
        P("groups", None),
        P("groups", None, None),
    )
    return jax.shard_map(
        shards,
        mesh=mesh,
        in_specs=placed,
        out_specs=P(("groups", "ctx", "fsdp"), None),
        check_vma=False,
    )
```

profile of v0, /device:TPU:31, one launch (start us, length us, event | category | flops | bytes accessed | tf_op | source)
XLA Modules:
  0.0 710.3 jit_solution(9324896033051884628)
XLA Ops:
  9.7 225.8 %all-gather.6.cloned.1.call-done = bf16[2048,4096]{1,0:T(8,128)(2,1)} async-done(((bf16[2048,512]{1,0:T(8,128)(2,1)}), bf16[2048,4096]{1,0:T(8,128)(2,1)}) %all-gather.6.cloned.1.call-update) | async-done | bytes 16777232 | tf_op jit(solution)/shard_map/all_gather | solution.py:151
  235.5 8.4 %convolution_convert_fusion = bf16[256,4096]{1,0:T(8,128)(2,1)S(1)} fusion(bf16[256,2048]{1,0:T(8,128)(2,1)S(1)} %copy-done, bf16[2048,4096]{1,0:T(8,128)(2,1)} %all-gather.6.cloned.1.call-done), kind=kOutput, calls=%fused_computation.35 | convolution fusion | flops 4296015872 | bytes 19922944 | tf_op jit(solution)/shard_map/dot_general | solution.py:149
  246.5 3.0 collective-permute-done
  250.9 2.8 divide_multiply_fusion
  257.3 3.5 fusion.45
  260.8 3.6 select_multiply_fusion
  266.6 2.7 fusion.88
  269.4 2.5 subtract_add_fusion
  278.7 2.5 fusion.90
  283.4 2.4 convolution_add_fusion.3
  289.3 4.5 fusion.34
  293.8 3.6 fusion.47
  297.4 3.9 fusion.40
  301.4 8.9 %fusion.46 = f32[4,16,128,128]{3,2,1,0:T(8,128)} fusion(f32[4,16,64,256]{3,2,1,0:T(8,128)S(1)} %fusion.34, f32[4,64,16,128]{3,1,0,2:T(8,128)S(1)} %bitcast.166, f32[4,16,64]{2,1,0:T(8,128)S(1)} %get-tuple-element.163), kind=kOutput, calls=%fused_computation.68 | convolution fusion | flops 805830656 | bytes 8421376 | tf_op jit(solution)/shard_map/...ck,...cv->...kv/dot_general | solution.py:112
  310.2 9.7 %multiply_subtract_fusion = f32[4,16,128,128]{3,2,1,0:T(8,128)} fusion(f32[128,128]{1,0:T(8,128)S(1)} %fusion.76, f32[4,16]{1,0:T(4,128)S(1)} %exp.36, f32[4,16,64,256]{3,2,1,0:T(8,128)S(1)} %fusion.34, f32[4,64,16,128]{3,1,0,2:T(8,128)S(1)} %bitcast.167, f32[4,16,64]{2,1,0:T(8,128)S(1)} %get-tuple-element.163), kind=kOutput, calls=%fused_computation.48 | convolution fusion | flops 807927808 | bytes 8488960 | tf_op jit(solution)/shard_map/...ck,...cj->...kj/dot_general | solution.py:109
  320.0 39.9 %while.30 = (s32[]{:T(128)}, f32[16,128,128]{2,1,0:T(8,128)S(1)}, f32[16,128,128]{2,1,0:T(8,128)S(1)}, f32[4,16,64,128]{3,2,0,1:T(8,128)}, f32[4,16,64,128]{3,2,...) while((s32[]{:T(128)}, f32[16,128,128]{2,1,0:T(8,128)S(1)}, ...), condition=%wide.region_4.5_spmd.clone, body=%wide.region_3.4_spmd.clone.sunk | while | flops 1208877056 | bytes 41423032 | solution.py:182
  324.7 2.9 fusion.157
  334.6 2.9 fusion.157
  344.6 2.9 fusion.157
  354.6 2.9 fusion.157
  361.7 126.7 %all-gather.8.cloned.1.call-done = f32[256,128,128]{2,1,0:T(8,128)} async-done(((f32[16,128,128]{2,1,0:T(8,128)}), f32[256,128,128]{2,1,0:T(8,128)}) %all-gather.8.cloned.1.call-update) | async-done | bytes 16777232 | tf_op jit(solution)/shard_map/all_gather | solution.py:22
  488.4 127.3 %all-gather.10.cloned.1.call-done = f32[256,128,128]{2,1,0:T(8,128)} async-done(((f32[16,128,128]{2,1,0:T(8,128)}), f32[256,128,128]{2,1,0:T(8,128)}) %all-gather.10.cloned.1.call-update) | async-done | bytes 16777232 | tf_op jit(solution)/shard_map/all_gather | solution.py:22
  615.9 80.2 %while.29 = (s32[]{:T(128)}, f32[16,128,128]{2,1,0:T(8,128)S(1)}, f32[16,128,128]{2,1,0:T(8,128)S(1)}, s32[]{:T(128)}, f32[16,16,128,128]{3,2,1,0:T(8,128)}, /*i...) while((s32[]{:T(128)}, f32[16,128,128]{2,1,0:T(8,128)S(1)}, ...), condition=%wide.region_6.7_spmd, body=%wide.region_5.6_spmd.sunk | while | flops 805568512 | bytes 11535499 | solution.py:30
  616.1 2.8 convolution_add_fusion.8
  618.9 2.4 fusion.146
  621.6 2.7 convolution_add_fusion.8
  624.3 2.4 fusion.146
  626.9 2.7 convolution_add_fusion.8
  632.2 2.7 convolution_add_fusion.8
  634.9 2.4 fusion.146
  637.5 2.7 convolution_add_fusion.8
  642.8 2.7 convolution_add_fusion.8
  645.5 2.4 fusion.146
  648.1 2.7 convolution_add_fusion.8
  653.5 2.7 convolution_add_fusion.8
  658.8 2.8 convolution_add_fusion.8
  661.6 2.4 fusion.146
  664.2 2.7 convolution_add_fusion.8
  669.5 2.7 convolution_add_fusion.8
  672.2 2.4 fusion.146
  674.9 2.7 convolution_add_fusion.8
  677.6 2.4 fusion.146
  680.2 2.7 convolution_add_fusion.8
  682.9 2.4 fusion.146
  685.5 2.7 convolution_add_fusion.8
  688.2 2.4 fusion.146
  690.8 2.7 convolution_add_fusion.8
  698.4 2.5 multiply_reduce_fusion
  (158 shorter events, 76.6 us)
Async XLA Ops:
  6.5 1.2 copy-start
  6.5 0.8 copy-start.15
  6.5 1.2 copy-start.9
  6.5 1.7 copy-start.13
  6.5 3.1 copy-start.10
  6.5 228.9 %all-gather.6.cloned.1.call-start = ((), (), s32[]{:S(2)}) async-start(), calls=%async_computation | async-start | bytes 18874368 | tf_op jit(solution)/shard_map/all_gather | solution.py:151
  7.3 481.1 %all-gather.8.cloned.1.call-start = ((), (), s32[]{:S(2)}) async-start(), calls=%async_computation.1 | async-start | bytes 17825792 | tf_op jit(solution)/shard_map/all_gather | solution.py:22
  9.7 239.8 %copy-start.11 = (bf16[3,4096]{1,0:T(4,128)(2,1)S(1)}, bf16[3,4096]{1,0:T(4,128)(2,1)}, u32[]{:S(2)}) copy-start(bf16[3,4096]{1,0:T(4,128)(2,1)} %param.20) | copy-start | bytes 73732
  244.5 5.0 collective-permute-start
  257.3 3.5 copy-start.12
  320.0 1.6 copy-start.5
  320.1 3.4 copy-start.2
  330.0 1.6 copy-start.5
  330.1 3.4 copy-start.2
  340.0 1.6 copy-start.5
  340.1 3.4 copy-start.2
  350.0 1.6 copy-start.5
  350.1 3.4 copy-start.2
  359.9 1.0 copy-start.3
  360.0 1.3 copy-start.4
  360.9 254.8 %all-gather.10.cloned.1.call-start = ((), (), s32[]{:S(2)}) async-start(), calls=%async_computation.2 | async-start | bytes 17825792 | tf_op jit(solution)/shard_map/all_gather | solution.py:22
  615.9 80.2 %copy-start.8 = (f32[16,128,128]{2,1,0:T(8,128)S(1)}, f32[16,128,128]{2,1,0:T(8,128)}, u32[]{:S(2)}) copy-start(f32[16,128,128]{2,1,0:T(8,128)} %param.21) | copy-start | bytes 3145732
  696.2 1.6 copy-start.6
  696.2 2.2 copy-start.7
  698.4 2.5 copy-start.14
  701.0 2.7 copy-start.1
Sparse Core Ops, SparseCore 0:
  9.4 226.0 all-gather.5
  361.1 127.2 all-gather.7
  490.6 125.0 all-gather.9
where the time goes:
time: 716 us; the launch traced here: 710 us
  waiting for transfers between devices  484 us (68%)
  matrix products  184 us (26%)
  local copies, waits for them, and re-layouts  16.5 us (2%)
  between operations  13.8 us (2%)
  other arithmetic  9.23 us (1%)
    all_gather x2, waiting for transfers between devices, entering(): gathered = jax.tree.map(lambda a: lax.all_gather(a, axis), part)  254 us
    all_gather x1, waiting for transfers between devices, shards(): lax.all_gather(qkv_weight, 'fsdp', axis=1, tiled=True)  226 us
    dot_general x15, matrix products, compose(): jnp.einsum('zom,zmg->zog', latter_piece[0], former_piece[1], precision=ex...  40.7 us
    dot_general x15, matrix products, compose(): jnp.einsum('hkj,hjm->hkm', latter_piece[0], former_piece[0], precision=ex...  36.3 us
  transfers between devices with their start and end apart: 4, of which 4 were waited for; matrix products, arithmetic and copies ran while one was open for 0% of the time, Pallas kernels for 0%

commit v1 on v0

--- a/solution.py
+++ b/solution.py
@@ -9,6 +9,22 @@
 DV = 128
 SPAN = 64
 exact_product = lax.Precision.HIGHEST
+
+
+def collect(x, axis, dim):
+    ways, here, lap = (lax.axis_size(axis), lax.axis_index(axis), x.shape[dim])
+    shape = [n * ways if d == dim else n for d, n in enumerate(x.shape)]
+    full = lax.dynamic_update_slice_in_dim(jnp.zeros(shape, x.dtype), x, here * lap, axis=dim)
+    going_up = going_down = x
+    for far in range(1, ways // 2 + 1):
+        going_up = lax.ppermute(going_up, axis, [(d, (d + 1) % ways) for d in range(ways)])
+        full = lax.dynamic_update_slice_in_dim(full, going_up, (here - far) % ways * lap, axis=dim)
+        if 2 * far < ways:
+            going_down = lax.ppermute(going_down, axis, [(d, (d - 1) % ways) for d in range(ways)])
+            full = lax.dynamic_update_slice_in_dim(
+                full, going_down, (here + far) % ways * lap, axis=dim
+            )
+    return full
 
 
 def shifted(array, axis, by):
@@ -147,9 +163,7 @@
     window_entry_state,
 ):
     mixed_qkv = jnp.dot(
-        hidden_in,
-        lax.all_gather(qkv_weight, "fsdp", axis=1, tiled=True),
-        preferred_element_type=jnp.float32,
+        hidden_in, collect(qkv_weight, "fsdp", 1), preferred_element_type=jnp.float32
     ).astype(jnp.bfloat16)
     gate_logits = jnp.dot(hidden_in, ab_weight, preferred_element_type=jnp.float32)
     tail_rows = previous_tail.shape[0]

time: 716 us -> 807 us (1.13)
  waiting for transfers between devices: 484 us -> 554 us
  local copies, waits for them, and re-layouts: 16.5 us -> 25 us
    ppermute x0 -> x7, waiting for transfers between devices: none -> 293 us  [the longest x4 293 us: collect(): lax.ppermute(going_up, axis, [(d, (d + 1) % ways) for d in range(ways)])]
    all_gather x1 -> x0, waiting for transfers between devices: 226 us -> none  [shards(): lax.all_gather(qkv_weight, 'fsdp', axis=1, tiled=True)]
    dynamic_update_slice x0 -> x8, local copies, waits for them, and re-layouts: none -> 12.3 us  [the longest x4 6.15 us: collect(): lax.dynamic_update_slice_in_dim(full, going_up, (here - far) % ways * lap...]
  transfers between devices with their start and end apart: 4 -> 10, of which waited for: 4 -> 8; matrix products, arithmetic and copies ran while one was open for 0% -> 2% of each run, Pallas kernels for 0% -> 0%
where the time goes in v1:
time: 807 us; the launch traced here: 799 us
  waiting for transfers between devices  554 us (69%)
  matrix products  188 us (23%)
  local copies, waits for them, and re-layouts  25 us (3%)
  between operations  14.4 us (2%)
  other arithmetic  10.7 us (1%)
    ppermute x4, waiting for transfers between devices, collect(): lax.ppermute(going_up, axis, [(d, (d + 1) % ways) for d in range(ways)])  293 us
    all_gather x2, waiting for transfers between devices, entering(): gathered = jax.tree.map(lambda a: lax.all_gather(a, axis), part)  257 us
    dot_general x15, matrix products, compose(): jnp.einsum('zom,zmg->zog', latter_piece[0], former_piece[1], precision=ex...  41.3 us
    dot_general x15, matrix products, compose(): jnp.einsum('hkj,hjm->hkm', latter_piece[0], former_piece[0], precision=ex...  35.7 us
  transfers between devices with their start and end apart: 10, of which 8 were waited for; matrix products, arithmetic and copies ran while one was open for 2% of the time, Pallas kernels for 0%

profile of v1, /device:TPU:31, one launch (start us, length us, event | category | flops | bytes accessed | tf_op | source)
XLA Modules:
  0.0 799.3 jit_solution(7994593494712777607)
XLA Ops:
  8.0 90.2 %collective-permute-done = bf16[2048,512]{1,0:T(8,128)(2,1)S(1)} collective-permute-done((bf16[2048,512]{1,0:T(8,128)(2,1)}, bf16[2048,512]{1,0:T(8,128)(2,1)S(1)}, u32[]{:S(2)}, u32[]{:S(2)}) %collective-permute-start) | collective-permute-done | bytes 2097184 | tf_op jit(solution)/shard_map/ppermute | solution.py:20
  100.5 88.3 %collective-permute-done.2 = bf16[2048,512]{1,0:T(8,128)(2,1)} collective-permute-done((bf16[2048,512]{1,0:T(8,128)(2,1)S(1)}, bf16[2048,512]{1,0:T(8,128)(2,1)}, u32[]{:S(2)}, u32[]{:S(2)}) %collective-permute-start.2) | collective-permute-done | bytes 2097184 | tf_op jit(solution)/shard_map/ppermute | solution.py:20
  195.5 83.2 %collective-permute-done.4 = bf16[2048,512]{1,0:T(8,128)(2,1)} collective-permute-done((bf16[2048,512]{1,0:T(8,128)(2,1)}, bf16[2048,512]{1,0:T(8,128)(2,1)}, u32[]{:S(2)}, u32[]{:S(2)}) %collective-permute-start.4) | collective-permute-done | bytes 2097184 | tf_op jit(solution)/shard_map/ppermute | solution.py:20
  291.3 31.5 %collective-permute-done.6 = bf16[2048,512]{1,0:T(8,128)(2,1)} collective-permute-done((bf16[2048,512]{1,0:T(8,128)(2,1)}, bf16[2048,512]{1,0:T(8,128)(2,1)}, u32[]{:S(2)}, u32[]{:S(2)}) %collective-permute-start.6) | collective-permute-done | bytes 2097184 | tf_op jit(solution)/shard_map/ppermute | solution.py:20
  324.7 4.7 fusion.31
  332.0 3.0 collective-permute-done.7
  336.4 3.0 divide_multiply_fusion
  342.6 3.5 fusion.46
  346.1 3.6 select_multiply_fusion
  352.0 2.4 fusion.89
  354.4 2.5 subtract_add_fusion
  359.1 2.4 convolution_add_fusion.4
  363.7 2.5 fusion.91
  368.4 2.4 convolution_add_fusion.3
  374.7 4.7 fusion.35
  379.4 3.6 fusion.48
  383.0 3.9 fusion.41
  387.0 8.9 %fusion.47 = f32[4,16,128,128]{3,2,1,0:T(8,128)} fusion(f32[4,16,64,256]{3,2,1,0:T(8,128)S(1)} %fusion.35, f32[4,64,16,128]{3,1,0,2:T(8,128)S(1)} %bitcast.168, f32[4,16,64]{2,1,0:T(8,128)S(1)} %get-tuple-element.163), kind=kOutput, calls=%fused_computation.69 | convolution fusion | flops 805830656 | bytes 8421376 | tf_op jit(solution)/shard_map/...ck,...cv->...kv/dot_general | solution.py:128
  395.9 9.4 %multiply_subtract_fusion = f32[4,16,128,128]{3,2,1,0:T(8,128)} fusion(f32[128,128]{1,0:T(8,128)S(1)} %fusion.77, f32[4,16]{1,0:T(4,128)S(1)} %exp.36, f32[4,16,64,256]{3,2,1,0:T(8,128)S(1)} %fusion.35, f32[4,64,16,128]{3,1,0,2:T(8,128)S(1)} %bitcast.169, f32[4,16,64]{2,1,0:T(8,128)S(1)} %get-tuple-element.163), kind=kOutput, calls=%fused_computation.49 | convolution fusion | flops 807927808 | bytes 8488960 | tf_op jit(solution)/shard_map/...ck,...cj->...kj/dot_general | solution.py:125
  405.4 39.6 %while.30 = (s32[]{:T(128)}, f32[16,128,128]{2,1,0:T(8,128)S(1)}, f32[16,128,128]{2,1,0:T(8,128)S(1)}, f32[4,16,64,128]{3,2,0,1:T(8,128)}, f32[4,16,64,128]{3,2,...) while((s32[]{:T(128)}, f32[16,128,128]{2,1,0:T(8,128)S(1)}, ...), condition=%wide.region_4.5_spmd.clone, body=%wide.region_3.4_spmd.clone.sunk | while | flops 1208877056 | bytes 33033364 | solution.py:196
  405.5 3.2 fusion.158
  411.2 2.9 fusion.157
  415.4 3.2 fusion.158
  421.1 2.9 fusion.157
  425.3 3.2 fusion.158
  431.0 2.9 fusion.157
  435.2 3.2 fusion.158
  440.9 2.9 fusion.157
  446.7 129.5 %all-gather.5.cloned.1.call-done = f32[256,128,128]{2,1,0:T(8,128)} async-done(((f32[16,128,128]{2,1,0:T(8,128)}), f32[256,128,128]{2,1,0:T(8,128)}) %all-gather.5.cloned.1.call-update) | async-done | bytes 16777232 | tf_op jit(solution)/shard_map/all_gather | solution.py:38
  576.2 127.3 %all-gather.7.cloned.1.call-done = f32[256,128,128]{2,1,0:T(8,128)} async-done(((f32[16,128,128]{2,1,0:T(8,128)}), f32[256,128,128]{2,1,0:T(8,128)}) %all-gather.7.cloned.1.call-update) | async-done | bytes 16777232 | tf_op jit(solution)/shard_map/all_gather | solution.py:38
  703.8 80.1 %while.29 = (s32[]{:T(128)}, f32[16,128,128]{2,1,0:T(8,128)S(1)}, f32[16,128,128]{2,1,0:T(8,128)S(1)}, s32[]{:T(128)}, f32[16,16,128,128]{3,2,1,0:T(8,128)}, /*i...) while((s32[]{:T(128)}, f32[16,128,128]{2,1,0:T(8,128)S(1)}, ...), condition=%wide.region_6.7_spmd, body=%wide.region_5.6_spmd.sunk | while | flops 805568512 | bytes 11535491 | solution.py:46
  703.9 2.8 convolution_add_fusion.8
  709.2 2.7 convolution_add_fusion.8
  714.6 2.7 convolution_add_fusion.8
  717.4 2.4 fusion.147
  719.9 2.7 convolution_add_fusion.8
  725.2 2.7 convolution_add_fusion.8
  730.5 2.7 convolution_add_fusion.8
  735.8 2.7 convolution_add_fusion.8
  741.1 2.8 convolution_add_fusion.8
  746.5 2.8 convolution_add_fusion.8
  751.9 2.7 convolution_add_fusion.8
  757.2 2.7 convolution_add_fusion.8
  762.5 2.7 convolution_add_fusion.8
  767.8 2.7 convolution_add_fusion.8
  773.1 2.7 convolution_add_fusion.8
  778.4 2.7 convolution_add_fusion.8
  785.5 4.0 multiply_reduce_fusion
  (162 shorter events, 100.8 us)
Async XLA Ops:
  6.5 182.9 %copy-start = (bf16[256,2048]{1,0:T(8,128)(2,1)S(1)}, bf16[256,2048]{1,0:T(8,128)(2,1)}, u32[]{:S(2)}) copy-start(bf16[256,2048]{1,0:T(8,128)(2,1)} %param.13) | copy-start | bytes 3145732
  6.5 569.7 %all-gather.5.cloned.1.call-start = ((), (), s32[]{:S(2)}) async-start(), calls=%async_computation | async-start | bytes 17825792 | tf_op jit(solution)/shard_map/all_gather | solution.py:38
  6.5 91.7 %collective-permute-start = (bf16[2048,512]{1,0:T(8,128)(2,1)}, bf16[2048,512]{1,0:T(8,128)(2,1)S(1)}, u32[]{:S(2)}, u32[]{:S(2)}) collective-permute-start(bf16[2048,512]{1,0:T(8,128)(2,1)} %param.14), channel_id=1, source_target_pairs={{0,1},{1,2},{2,3},{3,4},{4,5},{5,6},{6,7},{7,0},{8,9},{9,10},{10,1... | collective-permute-start | bytes 6291464 | tf_op jit(solution)/shard_map/ppermute | solution.py:20
  6.5 91.7 %collective-permute-start.1 = (bf16[2048,512]{1,0:T(8,128)(2,1)}, bf16[2048,512]{1,0:T(8,128)(2,1)}, u32[]{:S(2)}, u32[]{:S(2)}) collective-permute-start(bf16[2048,512]{1,0:T(8,128)(2,1)} %param.14), channel_id=1, source_target_pairs={{0,7},{1,0},{2,1},{3,2},{4,3},{5,4},{6,5},{7,6},{8,15},{9,8},{10,9... | collective-permute-start | bytes 6291464 | tf_op jit(solution)/shard_map/ppermute | solution.py:23
  98.2 90.6 %collective-permute-start.2 = (bf16[2048,512]{1,0:T(8,128)(2,1)S(1)}, bf16[2048,512]{1,0:T(8,128)(2,1)}, u32[]{:S(2)}, u32[]{:S(2)}) collective-permute-start(bf16[2048,512]{1,0:T(8,128)(2,1)S(1)} %collective-permute-done), channel_id=1, source_target_pairs={{0,1},{1,2},{2,3},{3,4},{4,5},{5,6},{6,7},{7,0},{8,9},{9,10},{10,1... | collective-permute-start | bytes 6291464 | tf_op jit(solution)/shard_map/ppermute | solution.py:20
  98.3 95.6 %collective-permute-start.3 = (bf16[2048,512]{1,0:T(8,128)(2,1)}, bf16[2048,512]{1,0:T(8,128)(2,1)}, u32[]{:S(2)}, u32[]{:S(2)}) collective-permute-start(bf16[2048,512]{1,0:T(8,128)(2,1)} %collective-permute-done.1), channel_id=1, source_target_pairs={{0,7},{1,0},{2,1},{3,2},{4,3},{5,4},{6,5},{7,6},{8,15},{9,8},{10,9... | collective-permute-start | bytes 6291464 | tf_op jit(solution)/shard_map/ppermute | solution.py:23
  188.8 89.9 %collective-permute-start.4 = (bf16[2048,512]{1,0:T(8,128)(2,1)}, bf16[2048,512]{1,0:T(8,128)(2,1)}, u32[]{:S(2)}, u32[]{:S(2)}) collective-permute-start(bf16[2048,512]{1,0:T(8,128)(2,1)} %collective-permute-done.2), channel_id=1, source_target_pairs={{0,1},{1,2},{2,3},{3,4},{4,5},{5,6},{6,7},{7,0},{8,9},{9,10},{10,1... | collective-permute-start | bytes 6291464 | tf_op jit(solution)/shard_map/ppermute | solution.py:20
  193.9 95.5 %collective-permute-start.5 = (bf16[2048,512]{1,0:T(8,128)(2,1)}, bf16[2048,512]{1,0:T(8,128)(2,1)}, u32[]{:S(2)}, u32[]{:S(2)}) collective-permute-start(bf16[2048,512]{1,0:T(8,128)(2,1)} %collective-permute-done.3), channel_id=1, source_target_pairs={{0,7},{1,0},{2,1},{3,2},{4,3},{5,4},{6,5},{7,6},{8,15},{9,8},{10,9... | collective-permute-start | bytes 6291464 | tf_op jit(solution)/shard_map/ppermute | solution.py:23
  278.7 44.0 %collective-permute-start.6 = (bf16[2048,512]{1,0:T(8,128)(2,1)}, bf16[2048,512]{1,0:T(8,128)(2,1)}, u32[]{:S(2)}, u32[]{:S(2)}) collective-permute-start(bf16[2048,512]{1,0:T(8,128)(2,1)} %collective-permute-done.4), channel_id=1, source_target_pairs={{0,1},{1,2},{2,3},{3,4},{4,5},{5,6},{6,7},{7,0},{8,9},{9,10},{10,1... | collective-permute-start | bytes 6291464 | tf_op jit(solution)/shard_map/ppermute | solution.py:20
  278.9 1.9 copy-start.6
  324.7 10.3 %copy-start.8 = (bf16[3,4096]{1,0:T(4,128)(2,1)S(1)}, bf16[3,4096]{1,0:T(4,128)(2,1)}, u32[]{:S(2)}) copy-start(bf16[3,4096]{1,0:T(4,128)(2,1)} %param.20) | copy-start | bytes 73732
  330.1 5.0 collective-permute-start.7
  342.6 3.5 copy-start.9
  405.4 3.3 copy-start.2
  415.3 3.3 copy-start.2
  425.2 3.3 copy-start.2
  435.1 3.3 copy-start.2
  445.0 1.0 copy-start.3
  445.0 1.3 copy-start.4
  446.0 257.6 %all-gather.7.cloned.1.call-start = ((), (), s32[]{:S(2)}) async-start(), calls=%async_computation.1 | async-start | bytes 17825792 | tf_op jit(solution)/shard_map/all_gather | solution.py:38
  703.8 80.1 %copy-start.7 = (f32[16,128,128]{2,1,0:T(8,128)S(1)}, f32[16,128,128]{2,1,0:T(8,128)}, u32[]{:S(2)}) copy-start(f32[16,128,128]{2,1,0:T(8,128)} %param.21) | copy-start | bytes 3145732
  783.9 1.6 copy-start.5
  785.5 4.1 copy-start.10
  789.5 2.7 copy-start.1
Sparse Core Ops, SparseCore 0:
  446.1 130.1 all-gather.4
  578.4 125.0 all-gather.6
